TPU v7x, 32 devices: a whole 2x2x4 slice. The times are simulated.
32 devices in a mesh: groups: 2 (over y), dp: 4 (over z), vocab: 4 (over x, core).
Axes of the slice: x: 2, y: 2, z: 4, core: 2. Of those that a mesh axis runs over, the one named last changes fastest.
Arguments:
- tokens_in: bfloat16 [128, 3584], P(('groups', 'dp')), parts along dimension 0, may hold values from -6 to 6
- attention: bfloat16 [128, 4096], P(('groups', 'dp'), 'vocab'), parts along dimension 0, may hold values from -6 to 6
- out_projection: bfloat16 [4096, 3584], P('vocab', 'dp'), may hold values from -0.09375 to 0.09375
- tangent: float32 [8192, 3584], P(('groups', 'vocab'), 'dp'), parts along dimension 0, may hold values from -0.09375 to 0.09375
- norm_gain: bfloat16 [3584], replicated, may hold values from 0.25 to 1.75
- head_weight: bfloat16 [3584, 8192], P(None, ('dp', 'vocab')), may hold values from -1 to 1
- lengths: int32 [8], P('groups'), parts along dimension 0, may hold values from 1 to 16, 32 in all
- sampled: int32 [128], P('groups'), parts along dimension 0, may hold values from 0 to 8191
Outputs:
- fisher_product: float32 [8192, 3584], P(('groups', 'vocab'), 'dp'), parts along dimension 0
- token_tangent: float32 [64], P(('groups', 'dp')), parts along dimension 0
There are 2 independent parts, one for each index of `groups`. A program takes and returns all parts, laid end to end along the dimension named above; an argument that names none is the same for every part. Nothing has to cross between parts.
Inputs may be any that keep to these rules, and one draw needn't show every extreme that they name: Slots 0 to lengths[i] - 1 of dp block i are live; the entries sum to 32.
All inputs are finite; a program needn't handle non-finite values.
Results may differ from a plain program's by a relative error of at most 0.0096.
Values may be sent and summed in bfloat16 or wider, within the bound.
A program may use at most 128 MiB of HBM per device.

v0:
```python
import jax
import jax.numpy as jnp
from jax import lax
from jax.sharding import PartitionSpec as P

SOFT_CAP = 30.0
EPSILON = 1e-06


def packed_slots(lengths, slot_count, total_live):
    block_ends = jnp.cumsum(lengths)
    block_starts = block_ends - lengths
    packed = jnp.arange(total_live, dtype=jnp.int32)
    owners = jnp.sum((block_ends[None, :] <= packed[:, None]).astype(jnp.int32), axis=1)
    owner_hits = owners[:, None] == jnp.arange(lengths.shape[0], dtype=jnp.int32)[None, :]
    first_slot = jnp.sum(jnp.where(owner_hits, block_starts[None, :], 0), axis=1)
    local_slot = packed - first_slot
    return (owners, local_slot, owners * slot_count + local_slot)


def local(tokens_in, attention, out_projection, tangent, norm_gain, head_weight, lengths, sampled):
    devices = lax.axis_size("dp")
    my_block = lax.axis_index("dp")
    slot_count = tokens_in.shape[0]
    live_dev = slot_count // 2
    total_live = live_dev * devices
    slots_all = slot_count * devices
    columns = head_weight.shape[1]
    column_start = (
        lax.axis_index("dp") * lax.axis_size("vocab") + lax.axis_index("vocab")
    ) * columns
    owners, local_slot, packed_slot = packed_slots(lengths, slot_count, total_live)
    slot_ids = jnp.arange(slots_all, dtype=jnp.int32)
    per_slot = jnp.repeat(lengths, slot_count, total_repeat_length=slots_all)
    all_weight = (slot_ids % slot_count < per_slot).astype(jnp.float32)
    tangent_narrow = tangent.astype(jnp.bfloat16)
    full_projection, full_tangent, all_attention = (
        lax.all_gather(out_projection, "dp", axis=1, tiled=True),
        lax.all_gather(tangent_narrow, "dp", axis=1, tiled=True),
        lax.all_gather(attention, "dp", axis=0, tiled=True),
    )
    partial_hidden = jnp.dot(attention, full_projection, preferred_element_type=jnp.float32)
    partial_tangent = jnp.dot(attention, full_tangent, preferred_element_type=jnp.float32)
    summed_hidden, tangent_hidden = lax.psum((partial_hidden, partial_tangent), "vocab")
    hidden = tokens_in.astype(jnp.float32) + summed_hidden
    gain_wide = norm_gain.astype(jnp.float32)
    scale_row = lax.rsqrt(jnp.mean(hidden * hidden, axis=1, keepdims=True) + EPSILON)
    normed = (gain_wide * hidden * scale_row).astype(jnp.bfloat16)
    inner_dot = jnp.mean(hidden * tangent_hidden, axis=1, keepdims=True)
    tangent_normed = (
        gain_wide * scale_row * (tangent_hidden - hidden * scale_row * scale_row * inner_dot)
    ).astype(jnp.bfloat16)
    stacked = jnp.stack([normed, tangent_normed])
    logits_pair = jnp.einsum(
        "srd,dc->src",
        lax.all_gather(stacked, "dp", axis=1, tiled=True),
        head_weight,
        preferred_element_type=jnp.float32,
    )
    squashed = jnp.tanh(logits_pair[0] / SOFT_CAP)
    capped = SOFT_CAP * squashed
    slopes = 1.0 - squashed * squashed
    tangent_capped = slopes * logits_pair[1]
    exp_values = jnp.exp(capped)
    column_ids = column_start + jnp.arange(columns, dtype=jnp.int32)
    id_hits = sampled[:, None] == column_ids[None, :]
    totals, weighted, picked = lax.psum(
        (
            jnp.sum(exp_values, axis=1),
            jnp.sum(exp_values * tangent_capped, axis=1),
            jnp.sum(jnp.where(id_hits, tangent_capped, 0.0), axis=1),
        ),
        ("dp", "vocab"),
    )
    tangent_mean = weighted / totals
    back_logits = (
        all_weight[:, None]
        * exp_values
        / totals[:, None]
        * (tangent_capped - tangent_mean[:, None])
        * slopes
    ).astype(jnp.bfloat16)
    block_rows = lax.slice_in_dim(back_logits, 0, attention.shape[0] * lax.axis_size("dp"), axis=0)
    partial_back = lax.psum_scatter(
        jnp.einsum("rc,dc->rd", block_rows, head_weight, preferred_element_type=jnp.float32),
        "dp",
        scatter_dimension=0,
        tiled=True,
    )
    back_normed = lax.psum(partial_back, "vocab")
    back_gain = gain_wide * back_normed
    inner_back = jnp.mean(hidden * back_gain, axis=1, keepdims=True)
    back_hidden = (
        scale_row * back_gain - hidden * scale_row * scale_row * scale_row * inner_back
    ).astype(jnp.bfloat16)
    back_columns = lax.all_to_all(back_hidden, "dp", split_axis=1, concat_axis=0, tiled=True)
    fisher_product = jnp.einsum(
        "rq,rd->qd", all_attention, back_columns, preferred_element_type=jnp.float32
    )
    token_all = picked - tangent_mean
    wanted = lax.dynamic_slice_in_dim(packed_slot, my_block * live_dev, live_dev)
    token_mine = jnp.sum(
        jnp.where(wanted[:, None] == slot_ids[None, :], token_all[None, :], 0.0), axis=1
    )
    return (fisher_product, token_mine)


def solution(mesh):
    return jax.shard_map(
        local,
        mesh=mesh,
        in_specs=(
            P(("groups", "dp"), None),
            P(("groups", "dp"), "vocab"),
            P("vocab", "dp"),
            P(("groups", "vocab"), "dp"),
            P(),
            P(None, ("dp", "vocab")),
            P("groups"),
            P("groups"),
        ),
        out_specs=(P(("groups", "vocab"), "dp"), P(("groups", "dp"))),
        check_vma=False,
    )
```

profile of v0, /device:TPU:0, one launch (start us, length us, event | category | flops | bytes accessed | tf_op | source)
XLA Modules:
  0.0 466.4 jit_solution(17010358820702704865)
XLA Ops:
  7.2 0.0 copy-start.3
  7.2 0.0 copy-start
  7.2 0.0 all-gather.5.cloned.1.call-start
  7.2 3.5 convert_element_type.35
  10.7 0.0 all-gather.5.cloned.1.call-update
  10.7 0.0 all-gather.3.cloned.1.call-start
  10.8 0.7 all-gather.3.cloned.1.call-update
  11.5 0.0 all-reduce.7.cloned.1.call-start
  11.5 0.0 copy-done.3
  11.5 0.7 fusion.24
  12.2 133.9 %all-gather.5.cloned.1.call-done = bf16[1024,3584]{1,0:T(8,128)(2,1)} async-done(((bf16[1024,896]{1,0:T(8,128)(2,1)}), bf16[1024,3584]{1,0:T(8,128)(2,1)}) %all-gather.5.cloned.1.call-update) | async-done | bytes 7340048 | tf_op jit(solution)/shard_map/all_gather | solution.py:39
  146.1 0.0 copy-done
  146.1 4.8 %fusion.26 = f32[16,3584]{1,0:T(8,128)} fusion(bf16[16,1024]{1,0:T(8,128)(2,1)S(1)} %copy-done, bf16[1024,3584]{1,0:T(8,128)(2,1)} %all-gather.5.cloned.1.call-done), kind=kOutput, calls=%fused_computation.56 | convolution fusion | flops 117440512 | bytes 7602176 | tf_op jit(solution)/shard_map/dot_general | solution.py:43
  150.9 0.0 copy-start.1
  150.9 127.4 %all-gather.3.cloned.1.call-done = bf16[1024,3584]{1,0:T(8,128)(2,1)} async-done(((bf16[1024,896]{1,0:T(8,128)(2,1)}), bf16[1024,3584]{1,0:T(8,128)(2,1)}) %all-gather.3.cloned.1.call-update) | async-done | bytes 7340048 | tf_op jit(solution)/shard_map/all_gather | solution.py:38
  278.4 4.8 %fusion.25 = f32[16,3584]{1,0:T(8,128)} fusion(bf16[16,1024]{1,0:T(8,128)(2,1)S(1)} %copy-done, bf16[1024,3584]{1,0:T(8,128)(2,1)} %all-gather.3.cloned.1.call-done), kind=kOutput, calls=%fused_computation.55 | convolution fusion | flops 117440512 | bytes 7602176 | tf_op jit(solution)/shard_map/dot_general | solution.py:42
  283.2 0.0 all-reduce.7.cloned.1.call-update
  283.2 0.0 reduce-scatter.2.cloned.1.call-start
  283.3 2.6 compare_convert_fusion
  285.9 28.6 %all-reduce.7.cloned.1.call-done = (f32[16,3584]{1,0:T(8,128)}, f32[16,3584]{1,0:T(8,128)}) async-done(((f32[16,3584]{1,0:T(8,128)}, f32[16,3584]{1,0:T(8,128)}), (f32[16,3584]{1,0:T(8,128)}, f32[16,3584]{1,0:T(8,128)})) %all-reduce.7.cloned.1.call-update) | async-done | bytes 458768 | tf_op jit(solution)/shard_map/psum | solution.py:44
  314.6 1.2 multiply_reduce_fusion.2
  315.8 1.1 fusion.8
  316.9 0.0 copy-start.4
  316.9 21.1 %all_gather.14 = bf16[2,64,3584]{2,1,0:T(8,128)(2,1)S(1)} all-gather(bf16[2,16,3584]{2,1,0:T(8,128)(2,1)S(1)} %pad_maximum_fusion), channel_id=1, replica_groups=mesh['groups'=2,'dp'=4,'vocab'=4] {'dp'}, dimensions={1}, use_global_device_ids=true | all-gather | bytes 1146880 | tf_op jit(solution)/shard_map/all_gather | solution.py:56
  338.0 2.7 fusion
  340.7 0.1 fusion.10
  340.8 0.0 copy-done.4
  340.8 0.2 select_reduce_fusion
  341.0 29.5 %all-reduce = (f32[64]{0:T(128)S(1)}, f32[64]{0:T(128)S(1)}, f32[64]{0:T(128)S(1)}) all-reduce(f32[64]{0:T(128)S(1)} %get-tuple-element.21, f32[64]{0:T(128)S(1)} %fusion.10, f32[64]{0:T(128)S(1)} %get-tuple-element.20), channel_id=1, replica_groups=mesh['groups'=2,'dp'=4,'vocab'=4] {'dp','vocab'}, use_global_device_ids=true, to_apply=%region_7.8 | all-reduce | flops 192 | bytes 1536 | tf_op jit(solution)/shard_map/psum | solution.py:67
  370.5 4.2 fusion.11
  374.7 0.0 reduce-scatter.2.cloned.1.call-update
  374.7 0.0 all-reduce.5.cloned.1.call-start
  374.8 0.2 reduce-window.10
  375.0 22.3 %reduce-scatter.2.cloned.1.call-done = f32[16,3584]{1,0:T(8,128)} async-done(((f32[64,3584]{1,0:T(8,128)}), f32[16,3584]{1,0:T(8,128)}) %reduce-scatter.2.cloned.1.call-update) | async-done | bytes 229392 | tf_op jit(solution)/shard_map/reduce_scatter | solution.py:84
  397.2 0.0 all-reduce.5.cloned.1.call-update
  397.3 0.1 convert_reduce_fusion
  397.4 0.1 select_reduce_fusion.2
  397.4 32.9 %all-reduce.5.cloned.1.call-done = f32[16,3584]{1,0:T(8,128)} async-done(((f32[16,3584]{1,0:T(8,128)}), f32[16,3584]{1,0:T(8,128)}) %all-reduce.5.cloned.1.call-update) | async-done | bytes 229392 | tf_op jit(solution)/shard_map/psum | solution.py:90
  430.3 1.1 multiply_reduce_fusion
  431.4 1.1 subtract_convert_fusion
  432.5 0.7 copy.17
  433.1 4.6 all-to-all-start
  437.7 0.1 dynamic_slice.3
  437.8 13.9 %all_gather.15 = bf16[64,1024]{1,0:T(8,128)(2,1)S(1)} all-gather(bf16[16,1024]{1,0:T(8,128)(2,1)S(1)} %copy-done), channel_id=1, replica_groups=mesh['groups'=2,'dp'=4,'vocab'=4] {'dp'}, dimensions={0}, use_global_device_ids=true | all-gather | bytes 163840 | tf_op jit(solution)/shard_map/all_gather | solution.py:40
  451.7 0.7 select_reduce_fusion.1
  452.4 0.0 all-to-all-done
  452.4 2.5 convolution_bitcast_fusion
  454.8 5.0 %copy.14 = f32[1024,896]{1,0:T(8,128)} copy(f32[1024,896]{0,1:T(8,128)} %convolution_bitcast_fusion) | data formatting | bytes 7340032
  (17 shorter events, 0.1 us)
Async XLA Ops:
  7.2 4.4 copy-start.3
  7.2 138.9 %copy-start = (bf16[16,1024]{1,0:T(8,128)(2,1)S(1)}, bf16[16,1024]{1,0:T(8,128)(2,1)}, u32[]{:S(2)}) copy-start(bf16[16,1024]{1,0:T(8,128)(2,1)} %param.11) | copy-start | bytes 98308
  7.2 138.9 %all-gather.5.cloned.1.call-start = ((), (), s32[]{:S(2)}) async-start(), calls=%async_computation.3 | async-start | bytes 9175040 | tf_op jit(solution)/shard_map/all_gather | solution.py:39
  10.7 267.7 %all-gather.3.cloned.1.call-start = ((), (), s32[]{:S(2)}) async-start(), calls=%async_computation.2 | async-start | bytes 9175040 | tf_op jit(solution)/shard_map/all_gather | solution.py:38
  11.5 303.1 %all-reduce.7.cloned.1.call-start = ((), (), s32[]{:S(2)}) async-start(), calls=%async_computation.6 | async-start | bytes 917504 | tf_op jit(solution)/shard_map/psum | solution.py:44
  150.9 132.4 %copy-start.2 = (bf16[3584]{0:T(1024)(128)(2,1)S(1)}, bf16[3584]{0:T(1024)(128)(2,1)}, u32[]{:S(2)}) copy-start(bf16[3584]{0:T(1024)(128)(2,1)} %param.14) | copy-start | bytes 21508
  150.9 132.4 %copy-start.5 = (pred[64]{0:T(512)(128)(4,1)S(1)}, pred[64]{0:T(512)(128)(4,1)}, u32[]{:S(2)}) copy-start(pred[64]{0:T(512)(128)(4,1)} %constant.131) | copy-start | bytes 196
  150.9 132.4 %copy-start.6 = (pred[64]{0:T(512)(128)(4,1)S(1)}, pred[64]{0:T(512)(128)(4,1)}, u32[]{:S(2)}) copy-start(pred[64]{0:T(512)(128)(4,1)} %constant.132) | copy-start | bytes 196
  150.9 132.4 %copy-start.7 = (pred[64]{0:T(512)(128)(4,1)S(1)}, pred[64]{0:T(512)(128)(4,1)}, u32[]{:S(2)}) copy-start(pred[64]{0:T(512)(128)(4,1)} %constant.133) | copy-start | bytes 196
  150.9 163.7 %copy-start.1 = (bf16[16,3584]{1,0:T(8,128)(2,1)S(1)}, bf16[16,3584]{1,0:T(8,128)(2,1)}, u32[]{:S(2)}) copy-start(bf16[16,3584]{1,0:T(8,128)(2,1)} %param.10) | copy-start | bytes 344068
  283.2 114.0 %reduce-scatter.2.cloned.1.call-start = ((), (), s32[]{:S(2)}) async-start(), calls=%async_computation.4 | async-start | bytes 1146880 | tf_op jit(solution)/shard_map/reduce_scatter | solution.py:84
  316.9 23.9 %copy-start.4 = (s32[64]{0:T(128)S(1)}, s32[64]{0:T(128)}, u32[]{:S(2)}) copy-start(s32[64]{0:T(128)} %param.17) | copy-start | bytes 772
  374.7 55.6 %all-reduce.5.cloned.1.call-start = ((), (), s32[]{:S(2)}) async-start(), calls=%async_computation.5 | async-start | bytes 458752 | tf_op jit(solution)/shard_map/psum | solution.py:90
  433.1 19.3 %all-to-all-start = ((bf16[16,4,896]{2,0,1:T(8,128)(2,1)}), bf16[16,4,896]{2,0,1:T(8,128)(2,1)S(1)}, u32[]{:S(2)}, u32[]{:S(2)}) async-start(bf16[16,4,896]{2,0,1:T(8,128)(2,1)} %bitcast.66), calls=%async_computation.1 | async-start | bytes 229376 | tf_op jit(solution)/shard_map/all_to_all | solution.py:96
Sparse Core Ops, SparseCore 0:
  10.8 135.1 all-gather.4
  147.7 130.6 all-gather.2
  283.4 31.1 all-reduce.6
  374.8 22.3 reduce-scatter.1
  399.5 30.7 all-reduce.4
where the time goes:
time: 467 us; the launch traced here: 466 us
  waiting for transfers between devices  346 us (74%)
  blocking collectives  64.5 us (14%)
  matrix products  19 us (4%)
  between operations  13.9 us (3%)
  other arithmetic  11.9 us (3%)
  local copies, waits for them, and re-layouts  6.45 us (1%)
  starting transfers between devices  4.8 us (1%)
    all_gather x1, waiting for transfers between devices, local(): lax.all_gather(tangent_narrow, 'dp', axis=1, tiled=True)  134 us
    all_gather x1, waiting for transfers between devices, local(): lax.all_gather(out_projection, 'dp', axis=1, tiled=True)  127 us
    psum x1, waiting for transfers between devices, local(): back_normed = lax.psum(partial_back, 'vocab')  32.9 us
    psum x1, blocking collectives, local(): lax.psum((jnp.sum(exp_values, axis=1), jnp.sum(exp_values * tangent_cappe...  29.5 us
    psum x1, waiting for transfers between devices, local(): lax.psum((partial_hidden, partial_tangent), 'vocab')  28.6 us
    reduce_scatter x1, waiting for transfers between devices, local(): lax.psum_scatter(jnp.einsum('rc,dc->rd', block_rows, head_weight, preferr...  22.3 us
    all_gather x1, blocking collectives, local(): lax.all_gather(stacked, 'dp', axis=1, tiled=True)  21.1 us
    all_gather x1, blocking collectives, local(): lax.all_gather(attention, 'dp', axis=0, tiled=True)  13.9 us
  transfers between devices with their start and end apart: 6, of which 5 were waited for; matrix products, arithmetic and copies ran while one was open for 2% of the time, Pallas kernels for 0%

commit v1 on v0

v1 whole, which is shorter than its diff:
```python
import functools

import jax
import jax.numpy as jnp
from jax import lax
from jax.experimental import pallas as pl
from jax.experimental.pallas import tpu as pltpu
from jax.sharding import PartitionSpec as P

SOFT_CAP = 30.0
EPSILON = 1e-06
MESH = pl.DeviceIdType.MESH
LANES = 128
ROWS = 8
F32 = jnp.float32
BF16 = jnp.bfloat16
HIGHEST = lax.Precision.HIGHEST
NT = (((1,), (1,)), ((), ()))


def fused_kernel(
    n_dp, n_vocab,
    lengths_ref, sampled_ref, gain_ref, tokens_hbm, attention_hbm, projection_hbm, tangent_hbm, head_hbm,
    packed_ref, back_ref, token_ref,
    tokens_own, tokens_send, tokens_all, attention_all, projection, tangent, tangent_narrow, head,
    hid_send, hid_all, tan_send, tan_all, norm_all, msg_all, stat_all, part_send, part_all, bh_all,
    local_sem, att_s, att_r, tok_s, tok_r, hid_s, hid_r, tan_s, tan_r, norm_s, norm_r,
    msg_s, msg_r, stat_s, stat_r, part_s, part_r, bh_s, bh_r,
):
    d, v = lax.axis_index("dp"), lax.axis_index("vocab")
    n_all = n_dp * n_vocab
    me = d * n_vocab + v
    slots = tokens_all.shape[1]
    wide = tokens_all.shape[2]
    live = n_vocab * ROWS
    model = wide * n_dp
    columns = head.shape[1]
    base = part_all.shape[2] - LANES

    loads = [
        pltpu.make_async_copy(attention_hbm, attention_all.at[d], local_sem.at[0]),
        pltpu.make_async_copy(tokens_hbm, tokens_own, local_sem.at[1]),
        pltpu.make_async_copy(projection_hbm, projection, local_sem.at[2]),
        pltpu.make_async_copy(tangent_hbm, tangent, local_sem.at[3]),
        pltpu.make_async_copy(head_hbm, head, local_sem.at[4]),
    ]
    for load in loads:
        load.start()

    def peer_of(step):
        peer = lax.rem(me + step, n_all)
        return peer, lax.div(peer, n_vocab), lax.rem(peer, n_vocab)

    barrier = pltpu.get_barrier_semaphore()

    @pl.loop(1, n_all)
    def _(step):
        _, pd, pv = peer_of(step)
        pl.semaphore_signal(barrier, inc=1, device_id={"dp": pd, "vocab": pv}, device_id_type=MESH)

    pl.semaphore_wait(barrier, n_all - 1)

    def along_dp(step):
        return lax.rem(d + step, n_dp)

    def att_copy(step):
        return pltpu.make_async_remote_copy(
            attention_hbm, attention_all.at[d], att_s.at[step], att_r.at[step],
            device_id={"dp": along_dp(step)}, device_id_type=MESH)

    def tok_copy(step):
        return pltpu.make_async_remote_copy(
            tokens_send.at[along_dp(step)], tokens_all.at[d], tok_s.at[step], tok_r.at[step],
            device_id={"dp": along_dp(step)}, device_id_type=MESH)

    for step in range(1, n_dp):
        att_copy(step).start()
    loads[1].wait()
    for block in range(n_dp):
        tokens_send[block] = tokens_own[:, block * wide : (block + 1) * wide]
    for step in range(1, n_dp):
        tok_copy(step).start()
    tokens_all[d] = tokens_send[d]

    slot_at = lax.broadcasted_iota(jnp.int32, (live, n_dp * slots), 1)
    row_at = lax.broadcasted_iota(jnp.int32, (live, n_dp * slots), 0)
    hit = jnp.zeros((live, n_dp * slots), jnp.bool_)
    start = jnp.int32(0)
    for block in range(n_dp):
        length = lengths_ref[block]
        place = slot_at - block * slots
        hit = hit | ((place >= 0) & (place < length) & (row_at == start + place))
        start = start + length
    pick = jnp.where(hit, 1.0, 0.0)
    pick_narrow = pick.astype(BF16)
    wanted = jnp.sum(pick * sampled_ref[...].astype(F32), axis=1, keepdims=True).astype(jnp.int32)

    gain = jnp.zeros((1, wide), F32)
    for block in range(n_dp):
        gain = jnp.where(d == block, gain_ref[:, block * wide : (block + 1) * wide].astype(F32), gain)

    loads[3].wait()
    tangent_narrow[...] = tangent[...].astype(BF16)
    loads[2].wait()
    loads[0].wait()
    for step in range(1, n_dp):
        att_copy(step).wait()
    everything = attention_all[...].reshape(n_dp * slots, attention_all.shape[2])
    packed = jnp.dot(pick_narrow, everything, preferred_element_type=F32).astype(BF16)
    packed_ref[...] = packed

    def along_vocab(step):
        return lax.rem(v + step, n_vocab)

    def chunk_copy(src, dst, send, recv):
        def copy(step):
            return pltpu.make_async_remote_copy(
                src.at[along_vocab(step)], dst.at[v], send.at[step], recv.at[step],
                device_id={"vocab": along_vocab(step)}, device_id_type=MESH)

        return copy

    hid_copy = chunk_copy(hid_send, hid_all, hid_s, hid_r)
    tan_copy = chunk_copy(tan_send, tan_all, tan_s, tan_r)
    hid_send[...] = jnp.dot(packed, projection[...], preferred_element_type=F32).reshape(n_vocab, ROWS, wide)
    for step in range(1, n_vocab):
        hid_copy(step).start()
    hid_all[v] = hid_send[v]
    tan_send[...] = jnp.dot(packed, tangent_narrow[...], preferred_element_type=F32).reshape(n_vocab, ROWS, wide)
    for step in range(1, n_vocab):
        tan_copy(step).start()
    tan_all[v] = tan_send[v]

    for step in range(1, n_dp):
        tok_copy(step).wait()
    my_slot = lax.broadcasted_iota(jnp.int32, (ROWS, live), 1)
    my_row = lax.broadcasted_iota(jnp.int32, (ROWS, live), 0) + v * ROWS
    own_rows = jnp.where(my_slot == my_row, 1.0, 0.0)
    own_pick = jnp.dot(own_rows.astype(BF16), pick_narrow, preferred_element_type=F32).astype(BF16)
    tokens = jnp.dot(
        own_pick, tokens_all[...].reshape(n_dp * slots, wide), preferred_element_type=F32
    )
    for step in range(1, n_vocab):
        hid_copy(step).wait()
    hidden = tokens + jnp.sum(hid_all[...], axis=0)
    for step in range(1, n_vocab):
        tan_copy(step).wait()
    tangent_hidden = jnp.sum(tan_all[...], axis=0)

    lane = lax.broadcasted_iota(jnp.int32, (ROWS, LANES), 1)
    squares = jnp.sum(hidden * hidden, axis=1, keepdims=True)
    cross = jnp.sum(hidden * tangent_hidden, axis=1, keepdims=True)
    norm_all[d] = jnp.where(lane < 1, squares, cross)

    def norm_copy(step):
        return pltpu.make_async_remote_copy(
            norm_all.at[d], norm_all.at[d], norm_s.at[step], norm_r.at[step],
            device_id={"dp": along_dp(step)}, device_id_type=MESH)

    for step in range(1, n_dp):
        norm_copy(step).start()
    for step in range(1, n_dp):
        norm_copy(step).wait()
    inverse = 1.0 / model
    means = jnp.sum(norm_all[...], axis=0) * inverse
    scale = lax.rsqrt(means[:, 0:1] + EPSILON)
    normed = gain * hidden * scale
    tangent_normed = gain * scale * (tangent_hidden - hidden * scale * scale * means[:, 1:2])
    msg_all[me] = jnp.concatenate([normed, tangent_normed], axis=0).astype(BF16)

    def to_all(src, dst, send, recv):
        def copy(step):
            _, pd, pv = peer_of(step)
            return pltpu.make_async_remote_copy(
                src(step), dst.at[me], send.at[step], recv.at[step],
                device_id={"dp": pd, "vocab": pv}, device_id_type=MESH)

        return copy

    def start_all(copy):
        @pl.loop(1, n_all)
        def _(step):
            copy(step).start()

    def wait_all(copy):
        @pl.loop(1, n_all)
        def _(step):
            copy(step).wait()

    msg_copy = to_all(lambda step: msg_all.at[me], msg_all, msg_s, msg_r)
    start_all(msg_copy)
    loads[4].wait()
    wait_all(msg_copy)

    pair = jnp.zeros((n_vocab * 2 * ROWS, columns), F32)
    for block in range(n_dp):
        pair = pair + jnp.dot(
            msg_all[block * n_vocab : (block + 1) * n_vocab].reshape(n_vocab * 2 * ROWS, wide),
            head[block * wide : (block + 1) * wide, :],
            preferred_element_type=F32,
        )
    pair = pair.reshape(n_vocab, 2 * ROWS, columns)
    logits = pair[:, 0:ROWS].reshape(live, columns)
    squashed = jnp.tanh(logits * (1.0 / SOFT_CAP))
    slopes = 1.0 - squashed * squashed
    tangent_capped = slopes * pair[:, ROWS:].reshape(live, columns)
    exp_values = jnp.exp(SOFT_CAP * squashed)
    column_at = lax.broadcasted_iota(jnp.int32, (live, columns), 1) + me * columns
    total = jnp.sum(exp_values, axis=1, keepdims=True)
    weighted = jnp.sum(exp_values * tangent_capped, axis=1, keepdims=True)
    picked = jnp.sum(jnp.where(column_at == wanted, tangent_capped, 0.0), axis=1, keepdims=True)
    stat_lane = lax.broadcasted_iota(jnp.int32, (live, LANES), 1)
    stats = (
        jnp.where(stat_lane == 0, total, 0.0)
        + jnp.where(stat_lane == 1, weighted, 0.0)
        + jnp.where(stat_lane == 2, picked, 0.0)
    )
    turn = jnp.where(
        lax.broadcasted_iota(jnp.int32, (ROWS, LANES), 0) == lax.broadcasted_iota(jnp.int32, (ROWS, LANES), 1), 1.0, 0.0
    )
    stat_all[me, :, 0:live] = lax.dot_general(turn, stats, NT, precision=HIGHEST, preferred_element_type=F32)
    if live < LANES:
        stat_all[me, :, live:] = jnp.zeros((ROWS, LANES - live), F32)
    stat_copy = to_all(lambda step: stat_all.at[me], stat_all, stat_s, stat_r)
    start_all(stat_copy)
    wait_all(stat_copy)
    across = jnp.sum(stat_all[...], axis=0)
    across = across[:, 0:live]
    mean_row = across[1:2] / across[0:1]
    token_ref[...] = across[2:3] - mean_row
    both = jnp.where(lax.broadcasted_iota(jnp.int32, (ROWS, live), 0) == 0, across[0:1], mean_row)
    square = jnp.where(
        lax.broadcasted_iota(jnp.int32, (live, live), 0) == lax.broadcasted_iota(jnp.int32, (live, live), 1), 1.0, 0.0
    )
    down = lax.dot_general(square, both, NT, precision=HIGHEST, preferred_element_type=F32)
    all_total, tangent_mean = down[:, 0:1], down[:, 1:2]

    back_logits = (exp_values / all_total * (tangent_capped - tangent_mean) * slopes).astype(BF16)
    inner_part = jnp.sum(back_logits.astype(F32) * logits, axis=1, keepdims=True)
    inner_tail = jnp.where(stat_lane == 0, inner_part, 0.0).reshape(n_vocab, ROWS, LANES)
    for block in range(n_dp):
        part_send[block * n_vocab : (block + 1) * n_vocab, :, 0:wide] = lax.dot_general(
            back_logits, head[block * wide : (block + 1) * wide, :], NT, preferred_element_type=F32
        ).reshape(n_vocab, ROWS, wide)
        part_send[block * n_vocab : (block + 1) * n_vocab, :, base:] = inner_tail

    def part_src(step):
        peer, _, _ = peer_of(step)
        return part_send.at[peer]

    part_copy = to_all(part_src, part_all, part_s, part_r)
    start_all(part_copy)
    part_all[me] = part_send[me]
    wait_all(part_copy)
    back_gain = gain * jnp.sum(part_all[:, :, 0:wide], axis=0)
    inner_back = jnp.sum(jnp.sum(part_all[:, :, base:], axis=0), axis=1, keepdims=True) * inverse
    bh_all[v] = scale * back_gain - hidden * (scale * scale * inner_back)

    def bh_copy(step):
        return pltpu.make_async_remote_copy(
            bh_all.at[v], bh_all.at[v], bh_s.at[step], bh_r.at[step],
            device_id={"vocab": along_vocab(step)}, device_id_type=MESH)

    for step in range(1, n_vocab):
        bh_copy(step).start()
    for step in range(1, n_vocab):
        bh_copy(step).wait()
    back_ref[...] = bh_all[...].reshape(live, wide).astype(BF16)


def local(n_dp, n_vocab, tokens_in, attention, out_projection, tangent, norm_gain, head_weight, lengths, sampled):
    slots, model = tokens_in.shape
    features, wide = out_projection.shape
    columns = head_weight.shape[1]
    live_dev = slots // 2
    live = live_dev * n_dp
    assert live == n_vocab * ROWS and live <= LANES
    n_all = n_dp * n_vocab
    padded = -(-wide // LANES) * LANES + LANES
    vmem, anywhere = pl.BlockSpec(memory_space=pltpu.VMEM), pl.BlockSpec(memory_space=pl.ANY)
    dma = pltpu.SemaphoreType.DMA
    packed, back, token_all = pl.pallas_call(
        functools.partial(fused_kernel, n_dp, n_vocab),
        out_shape=(
            jax.ShapeDtypeStruct((live, features), BF16),
            jax.ShapeDtypeStruct((live, wide), BF16),
            jax.ShapeDtypeStruct((1, live), F32),
        ),
        in_specs=[pl.BlockSpec(memory_space=pltpu.SMEM), vmem, vmem] + [anywhere] * 5,
        out_specs=(vmem, vmem, vmem),
        scratch_shapes=[
            pltpu.VMEM((slots, model), BF16),
            pltpu.VMEM((n_dp, slots, wide), BF16),
            pltpu.VMEM((n_dp, slots, wide), BF16),
            pltpu.VMEM((n_dp, slots, features), BF16),
            pltpu.VMEM((features, wide), BF16),
            pltpu.VMEM((features, wide), F32),
            pltpu.VMEM((features, wide), BF16),
            pltpu.VMEM((model, columns), BF16),
            pltpu.VMEM((n_vocab, ROWS, wide), F32),
            pltpu.VMEM((n_vocab, ROWS, wide), F32),
            pltpu.VMEM((n_vocab, ROWS, wide), F32),
            pltpu.VMEM((n_vocab, ROWS, wide), F32),
            pltpu.VMEM((n_dp, ROWS, LANES), F32),
            pltpu.VMEM((n_all, 2 * ROWS, wide), BF16),
            pltpu.VMEM((n_all, ROWS, LANES), F32),
            pltpu.VMEM((n_all, ROWS, padded), F32),
            pltpu.VMEM((n_all, ROWS, padded), F32),
            pltpu.VMEM((n_vocab, ROWS, wide), F32),
            dma((5,)),
            dma((n_dp,)), dma((n_dp,)), dma((n_dp,)), dma((n_dp,)),
            dma((n_vocab,)), dma((n_vocab,)), dma((n_vocab,)), dma((n_vocab,)),
            dma((n_dp,)), dma((n_dp,)),
            dma((n_all,)), dma((n_all,)), dma((n_all,)), dma((n_all,)), dma((n_all,)), dma((n_all,)),
            dma((n_vocab,)), dma((n_vocab,)),
        ],
        compiler_params=pltpu.CompilerParams(
            collective_id=0, has_side_effects=True, vmem_limit_bytes=40 * 1024 * 1024
        ),
    )(lengths, sampled.reshape(1, -1), norm_gain.reshape(1, -1),
      tokens_in, attention, out_projection, tangent, head_weight)
    fisher_product = lax.dot_general(packed, back, (((0,), (0,)), ((), ())), preferred_element_type=F32)
    token_mine = lax.dynamic_slice_in_dim(token_all[0], lax.axis_index("dp") * live_dev, live_dev)
    return (fisher_product, token_mine)


def solution(mesh):
    return jax.shard_map(
        functools.partial(local, mesh.shape["dp"], mesh.shape["vocab"]),
        mesh=mesh,
        in_specs=(
            P(("groups", "dp"), None),
            P(("groups", "dp"), "vocab"),
            P("vocab", "dp"),
            P(("groups", "vocab"), "dp"),
            P(),
            P(None, ("dp", "vocab")),
            P("groups"),
            P("groups"),
        ),
        out_specs=(P(("groups", "vocab"), "dp"), P(("groups", "dp"))),
        check_vma=False,
    )
```

time: 467 us -> 66.8 us (0.14)
  waiting for transfers between devices: 346 us -> 0 us
  blocking collectives: 64.5 us -> 0 us
  Pallas kernels: 0 us -> 53.2 us
  matrix products: 19 us -> 2.49 us
  between operations: 13.9 us -> 0.66 us
  other arithmetic: 11.9 us -> 0 us
  starting transfers between devices: 4.8 us -> 0 us
    all_gather x2 -> x0, waiting for transfers between devices: 261 us -> none  [the longest x1 134 us: local(): lax.all_gather(tangent_narrow, 'dp', axis=1, tiled=True)]
    psum x2 -> x0, waiting for transfers between devices: 61.5 us -> none  [the longest x1 32.9 us: local(): back_normed = lax.psum(partial_back, 'vocab')]
    pallas_call x0 -> x1, Pallas kernels: none -> 53.2 us  [local(): pl.pallas_call(functools.partial(fused_kernel, n_dp, n_vocab), out_shape=...]
    all_gather x2 -> x0, blocking collectives: 35 us -> none  [the longest x1 21.1 us: local(): lax.all_gather(stacked, 'dp', axis=1, tiled=True)]
    psum x1 -> x0, blocking collectives: 29.5 us -> none  [local(): lax.psum((jnp.sum(exp_values, axis=1), jnp.sum(exp_values * tangent_cappe...]
    reduce_scatter x1 -> x0, waiting for transfers between devices: 22.3 us -> none  [local(): lax.psum_scatter(jnp.einsum('rc,dc->rd', block_rows, head_weight, preferr...]
    dot_general x5 -> x1, matrix products: 19 us -> 2.49 us  [local(): lax.dot_general(packed, back, (((0,), (0,)), ((), ())), preferred_element...]
    convert_element_type x4 -> x0, other arithmetic: 7.12 us -> none  [the longest x1 3.46 us: local(): tangent_narrow = tangent.astype(jnp.bfloat16)]
  transfers between devices with their start and end apart: 6 -> 0, of which waited for: 5 -> 0; matrix products, arithmetic and copies ran while one was open for 2% -> 0% of each run, Pallas kernels for 0% -> 0%
where the time goes in v1:
time: 66.8 us; the launch traced here: 66.1 us
  Pallas kernels  53.2 us (80%)
  local copies, waits for them, and re-layouts  9.83 us (15%)
  matrix products  2.49 us (4%)
    pallas_call x1, Pallas kernels, local(): pl.pallas_call(functools.partial(fused_kernel, n_dp, n_vocab), out_shape=...  53.2 us
    unnamed x14, local copies, waits for them, and re-layouts  8.54 us
    dot_general x1, matrix products, local(): lax.dot_general(packed, back, (((0,), (0,)), ((), ())), preferred_element...  2.49 us

profile of v1, /device:TPU:0, one launch (start us, length us, event | category | flops | bytes accessed | tf_op | source)
XLA Modules:
  0.0 66.1 jit_solution(17446524741032227610)
XLA Ops:
  0.6 0.7 %reshape.12.gain_ref = bf16[1,3584]{1,0:T(2,128)(2,1)S(1)} reshape(bf16[3584]{0:T(1024)(128)(2,1)} %param.12) | data formatting | bytes 14336 | tf_op jit(solution)/shard_map/reshape | solution.py:320
  1.3 0.0 copy-start
  1.4 2.0 %copy-done = f32[1024,896]{1,0:T(8,128)S(1)} copy-done((f32[1024,896]{1,0:T(8,128)S(1)}, f32[1024,896]{1,0:T(8,128)}, u32[]{:S(2)}) %copy-start) | copy-done | bytes 3670040
  3.4 0.0 copy-start.1
  3.4 2.0 %copy-done.1 = bf16[3584,512]{1,0:T(8,128)(2,1)S(1)} copy-done((bf16[3584,512]{1,0:T(8,128)(2,1)S(1)}, bf16[3584,512]{1,0:T(8,128)(2,1)}, u32[]{:S(2)}) %copy-start.1) | copy-done | bytes 3670040
  5.4 0.0 copy-start.2
  5.4 1.5 %copy-done.2 = bf16[1024,896]{1,0:T(8,128)(2,1)S(1)} copy-done((bf16[1024,896]{1,0:T(8,128)(2,1)S(1)}, bf16[1024,896]{1,0:T(8,128)(2,1)}, u32[]{:S(2)}) %copy-start.2) | copy-done | bytes 1835032
  6.9 0.0 copy-start.3
  6.9 0.9 %copy-done.3 = bf16[16,3584]{1,0:T(8,128)(2,1)S(1)} copy-done((bf16[16,3584]{1,0:T(8,128)(2,1)S(1)}, bf16[16,3584]{1,0:T(8,128)(2,1)}, u32[]{:S(2)}) %copy-start.3) | copy-done | bytes 114712
  7.8 0.0 copy-start.4
  7.8 0.8 %copy-done.4 = bf16[16,1024]{1,0:T(8,128)(2,1)S(1)} copy-done((bf16[16,1024]{1,0:T(8,128)(2,1)S(1)}, bf16[16,1024]{1,0:T(8,128)(2,1)}, u32[]{:S(2)}) %copy-start.4) | copy-done | bytes 32792
  8.6 0.0 copy-start.5
  8.6 0.7 copy-done.5
  9.2 0.0 copy-start.6
  9.2 0.7 copy-done.6
  9.9 53.2 %shard_map.95 = (bf16[32,1024]{1,0:T(8,128)(2,1)S(1)}, bf16[32,896]{1,0:T(8,128)(2,1)S(1)}, f32[1,32]{1,0:T(1,128)S(1)}) custom-call(s32[4]{0:T(128)S(1)} %copy-done.5, s32[1,64]{1,0:T(1,128)S(1)} %bitcast.5, bf16[1,3584]{1,0:T(2,128)(2,1)S(1)} %reshape.12.gain_ref, bf16[16,3584]{1,0:T(8,128)(2,1)S(1)} %copy-done.3, bf16[16,1024]{1,0:T(8,128)(2,1)S(1)} %copy-done.4, ...), custom_call_target="tpu_custom_call" | custom-call | tf_op jit(solution)/shard_map/pallas_call | solution.py:282
  63.1 0.6 dynamic-slice_bitcast_fusion
  63.7 2.5 %fusion = f32[1024,896]{1,0:T(8,128)} fusion(bf16[32,1024]{1,0:T(8,128)(2,1)S(1)} %get-tuple-element.5, bf16[32,896]{1,0:T(8,128)(2,1)S(1)} %get-tuple-element.6), kind=kOutput, calls=%fused_computation.1 | convolution fusion | flops 58720256 | bytes 3792896 | tf_op jit(solution)/shard_map/dot_general | solution.py:322
Async XLA Ops:
  1.3 2.0 %copy-start = (f32[1024,896]{1,0:T(8,128)S(1)}, f32[1024,896]{1,0:T(8,128)}, u32[]{:S(2)}) copy-start(f32[1024,896]{1,0:T(8,128)} %tangent_hbm.1) | copy-start | bytes 11010052
  3.4 2.0 %copy-start.1 = (bf16[3584,512]{1,0:T(8,128)(2,1)S(1)}, bf16[3584,512]{1,0:T(8,128)(2,1)}, u32[]{:S(2)}) copy-start(bf16[3584,512]{1,0:T(8,128)(2,1)} %head_hbm.1) | copy-start | bytes 11010052
  5.4 1.5 %copy-start.2 = (bf16[1024,896]{1,0:T(8,128)(2,1)S(1)}, bf16[1024,896]{1,0:T(8,128)(2,1)}, u32[]{:S(2)}) copy-start(bf16[1024,896]{1,0:T(8,128)(2,1)} %projection_hbm.1) | copy-start | bytes 5505028
  6.9 0.9 %copy-start.3 = (bf16[16,3584]{1,0:T(8,128)(2,1)S(1)}, bf16[16,3584]{1,0:T(8,128)(2,1)}, u32[]{:S(2)}) copy-start(bf16[16,3584]{1,0:T(8,128)(2,1)} %tokens_hbm.1) | copy-start | bytes 344068
  7.8 0.8 %copy-start.4 = (bf16[16,1024]{1,0:T(8,128)(2,1)S(1)}, bf16[16,1024]{1,0:T(8,128)(2,1)}, u32[]{:S(2)}) copy-start(bf16[16,1024]{1,0:T(8,128)(2,1)} %attention_hbm.1) | copy-start | bytes 98308
  8.6 0.7 copy-start.5
  9.2 0.7 copy-start.6

commit v2 on v1

--- a/solution.py
+++ b/solution.py
@@ -14,18 +14,17 @@
 ROWS = 8
 F32 = jnp.float32
 BF16 = jnp.bfloat16
-HIGHEST = lax.Precision.HIGHEST
 NT = (((1,), (1,)), ((), ()))
 
 
 def fused_kernel(
     n_dp, n_vocab,
-    lengths_ref, sampled_ref, gain_ref, tokens_hbm, attention_hbm, projection_hbm, tangent_hbm, head_hbm,
+    lengths_hbm, sampled_hbm, gain_hbm, tokens_hbm, attention_hbm, projection_hbm, tangent_hbm, head_hbm,
     packed_ref, back_ref, token_ref,
-    tokens_own, tokens_send, tokens_all, attention_all, projection, tangent, tangent_narrow, head,
+    lengths_ref, sampled_ref, gain_ref, tokens_own, tokens_send, tokens_all, attention_all, projection, tangent, tangent_narrow, head,
     hid_send, hid_all, tan_send, tan_all, norm_all, msg_all, stat_all, part_send, part_all, bh_all,
     local_sem, att_s, att_r, tok_s, tok_r, hid_s, hid_r, tan_s, tan_r, norm_s, norm_r,
-    msg_s, msg_r, stat_s, stat_r, part_s, part_r, bh_s, bh_r,
+    msg_s, msg_r, pass_s, pass_r, stat_s, stat_r, part_s, part_r, bh_s, bh_r,
 ):
     d, v = lax.axis_index("dp"), lax.axis_index("vocab")
     n_all = n_dp * n_vocab
@@ -42,6 +41,9 @@
         pltpu.make_async_copy(tokens_hbm, tokens_own, local_sem.at[1]),
         pltpu.make_async_copy(projection_hbm, projection, local_sem.at[2]),
         pltpu.make_async_copy(tangent_hbm, tangent, local_sem.at[3]),
+        pltpu.make_async_copy(lengths_hbm, lengths_ref, local_sem.at[5]),
+        pltpu.make_async_copy(sampled_hbm, sampled_ref, local_sem.at[6]),
+        pltpu.make_async_copy(gain_hbm, gain_ref, local_sem.at[7]),
         pltpu.make_async_copy(head_hbm, head, local_sem.at[4]),
     ]
     for load in loads:
@@ -51,18 +53,19 @@
         peer = lax.rem(me + step, n_all)
         return peer, lax.div(peer, n_vocab), lax.rem(peer, n_vocab)
 
-    barrier = pltpu.get_barrier_semaphore()
-
-    @pl.loop(1, n_all)
-    def _(step):
-        _, pd, pv = peer_of(step)
-        pl.semaphore_signal(barrier, inc=1, device_id={"dp": pd, "vocab": pv}, device_id_type=MESH)
-
-    pl.semaphore_wait(barrier, n_all - 1)
-
     def along_dp(step):
         return lax.rem(d + step, n_dp)
 
+    def along_vocab(step):
+        return lax.rem(v + step, n_vocab)
+
+    barrier = pltpu.get_barrier_semaphore()
+    for step in range(1, n_dp):
+        pl.semaphore_signal(barrier, inc=1, device_id={"dp": along_dp(step)}, device_id_type=MESH)
+    for step in range(1, n_vocab):
+        pl.semaphore_signal(barrier, inc=1, device_id={"vocab": along_vocab(step)}, device_id_type=MESH)
+    pl.semaphore_wait(barrier, n_dp + n_vocab - 2)
+
     def att_copy(step):
         return pltpu.make_async_remote_copy(
             attention_hbm, attention_all.at[d], att_s.at[step], att_r.at[step],
@@ -81,6 +84,9 @@
     for step in range(1, n_dp):
         tok_copy(step).start()
     tokens_all[d] = tokens_send[d]
+
+    for load in loads[4:7]:
+        load.wait()
 
     slot_at = lax.broadcasted_iota(jnp.int32, (live, n_dp * slots), 1)
     row_at = lax.broadcasted_iota(jnp.int32, (live, n_dp * slots), 0)
@@ -108,9 +114,6 @@
     everything = attention_all[...].reshape(n_dp * slots, attention_all.shape[2])
     packed = jnp.dot(pick_narrow, everything, preferred_element_type=F32).astype(BF16)
     packed_ref[...] = packed
-
-    def along_vocab(step):
-        return lax.rem(v + step, n_vocab)
 
     def chunk_copy(src, dst, send, recv):
         def copy(step):
@@ -187,10 +190,31 @@
         def _(step):
             copy(step).wait()
 
-    msg_copy = to_all(lambda step: msg_all.at[me], msg_all, msg_s, msg_r)
-    start_all(msg_copy)
-    loads[4].wait()
-    wait_all(msg_copy)
+    mate = v + 1 - 2 * lax.rem(v, 2)
+
+    def msg_copy(step):
+        _, pd, pv = peer_of(2 * step)
+        return pltpu.make_async_remote_copy(
+            msg_all.at[me], msg_all.at[me], msg_s.at[step], msg_r.at[step],
+            device_id={"dp": pd, "vocab": pv}, device_id_type=MESH)
+
+    def pass_copy(step):
+        came_from = lax.rem(me + n_all - 2 * step, n_all)
+        return pltpu.make_async_remote_copy(
+            msg_all.at[came_from], msg_all.at[came_from], pass_s.at[step], pass_r.at[step],
+            device_id={"vocab": mate}, device_id_type=MESH)
+
+    for step in range(1, n_all // 2):
+        msg_copy(step).start()
+    pass_copy(0).start()
+    loads[7].wait()
+    for step in range(1, n_all // 2):
+        msg_copy(step).wait_recv()
+        pass_copy(step).start()
+    for step in range(1, n_all // 2):
+        msg_copy(step).wait_send()
+    for step in range(n_all // 2):
+        pass_copy(step).wait()
 
     pair = jnp.zeros((n_vocab * 2 * ROWS, columns), F32)
     for block in range(n_dp):
@@ -215,34 +239,37 @@
         + jnp.where(stat_lane == 1, weighted, 0.0)
         + jnp.where(stat_lane == 2, picked, 0.0)
     )
-    turn = jnp.where(
-        lax.broadcasted_iota(jnp.int32, (ROWS, LANES), 0) == lax.broadcasted_iota(jnp.int32, (ROWS, LANES), 1), 1.0, 0.0
-    )
-    stat_all[me, :, 0:live] = lax.dot_general(turn, stats, NT, precision=HIGHEST, preferred_element_type=F32)
     if live < LANES:
-        stat_all[me, :, live:] = jnp.zeros((ROWS, LANES - live), F32)
+        stats = jnp.concatenate([stats, jnp.zeros((LANES - live, LANES), F32)], axis=0)
+    stat_all[me] = stats.T[0:ROWS]
     stat_copy = to_all(lambda step: stat_all.at[me], stat_all, stat_s, stat_r)
     start_all(stat_copy)
     wait_all(stat_copy)
     across = jnp.sum(stat_all[...], axis=0)
-    across = across[:, 0:live]
-    mean_row = across[1:2] / across[0:1]
-    token_ref[...] = across[2:3] - mean_row
-    both = jnp.where(lax.broadcasted_iota(jnp.int32, (ROWS, live), 0) == 0, across[0:1], mean_row)
-    square = jnp.where(
-        lax.broadcasted_iota(jnp.int32, (live, live), 0) == lax.broadcasted_iota(jnp.int32, (live, live), 1), 1.0, 0.0
-    )
-    down = lax.dot_general(square, both, NT, precision=HIGHEST, preferred_element_type=F32)
-    all_total, tangent_mean = down[:, 0:1], down[:, 1:2]
+    across = jnp.concatenate([across, jnp.zeros((LANES - ROWS, LANES), F32)], axis=0).T[0:live]
+    all_total = across[:, 0:1]
+    tangent_mean = across[:, 1:2] / all_total
+    token = across[:, 2:3] - tangent_mean
+    token_row = lax.broadcasted_iota(jnp.int32, (live, slots // 2), 0)
+    token_lane = lax.broadcasted_iota(jnp.int32, (live, slots // 2), 1) + d * (slots // 2)
+    token_ref[...] = jnp.sum(jnp.where(token_row == token_lane, token, 0.0), axis=0, keepdims=True)
 
     back_logits = (exp_values / all_total * (tangent_capped - tangent_mean) * slopes).astype(BF16)
     inner_part = jnp.sum(back_logits.astype(F32) * logits, axis=1, keepdims=True)
-    inner_tail = jnp.where(stat_lane == 0, inner_part, 0.0).reshape(n_vocab, ROWS, LANES)
-    for block in range(n_dp):
-        part_send[block * n_vocab : (block + 1) * n_vocab, :, 0:wide] = lax.dot_general(
+    high = inner_part.astype(BF16).astype(F32)
+    middle = (inner_part - high).astype(BF16).astype(F32)
+    low = inner_part - high - middle
+    inner_tail = (
+        jnp.where(stat_lane == 0, high, 0.0)
+        + jnp.where(stat_lane == 1, middle, 0.0)
+        + jnp.where(stat_lane == 2, low, 0.0)
+    ).reshape(n_vocab, ROWS, LANES)
+    for block in range(n_dp):
+        part = lax.dot_general(
             back_logits, head[block * wide : (block + 1) * wide, :], NT, preferred_element_type=F32
         ).reshape(n_vocab, ROWS, wide)
-        part_send[block * n_vocab : (block + 1) * n_vocab, :, base:] = inner_tail
+        part_send[block * n_vocab : (block + 1) * n_vocab, :, 0:wide] = part.astype(BF16)
+        part_send[block * n_vocab : (block + 1) * n_vocab, :, base:] = inner_tail.astype(BF16)
 
     def part_src(step):
         peer, _, _ = peer_of(step)
@@ -252,9 +279,9 @@
     start_all(part_copy)
     part_all[me] = part_send[me]
     wait_all(part_copy)
-    back_gain = gain * jnp.sum(part_all[:, :, 0:wide], axis=0)
-    inner_back = jnp.sum(jnp.sum(part_all[:, :, base:], axis=0), axis=1, keepdims=True) * inverse
-    bh_all[v] = scale * back_gain - hidden * (scale * scale * inner_back)
+    back_gain = gain * jnp.sum(part_all[:, :, 0:wide].astype(F32), axis=0)
+    inner_back = jnp.sum(jnp.sum(part_all[:, :, base:].astype(F32), axis=0), axis=1, keepdims=True) * inverse
+    bh_all[v] = (scale * back_gain - hidden * (scale * scale * inner_back)).astype(BF16)
 
     def bh_copy(step):
         return pltpu.make_async_remote_copy(
@@ -265,7 +292,7 @@
         bh_copy(step).start()
     for step in range(1, n_vocab):
         bh_copy(step).wait()
-    back_ref[...] = bh_all[...].reshape(live, wide).astype(BF16)
+    back_ref[...] = bh_all[...].astype(F32).reshape(live, wide).astype(BF16)
 
 
 def local(n_dp, n_vocab, tokens_in, attention, out_projection, tangent, norm_gain, head_weight, lengths, sampled):
@@ -277,18 +304,21 @@
     assert live == n_vocab * ROWS and live <= LANES
     n_all = n_dp * n_vocab
     padded = -(-wide // LANES) * LANES + LANES
-    vmem, anywhere = pl.BlockSpec(memory_space=pltpu.VMEM), pl.BlockSpec(memory_space=pl.ANY)
+    vmem, hbm = pl.BlockSpec(memory_space=pltpu.VMEM), pl.BlockSpec(memory_space=pltpu.HBM)
     dma = pltpu.SemaphoreType.DMA
-    packed, back, token_all = pl.pallas_call(
+    packed, back, token_mine = pl.pallas_call(
         functools.partial(fused_kernel, n_dp, n_vocab),
         out_shape=(
             jax.ShapeDtypeStruct((live, features), BF16),
             jax.ShapeDtypeStruct((live, wide), BF16),
-            jax.ShapeDtypeStruct((1, live), F32),
+            jax.ShapeDtypeStruct((1, live_dev), F32),
         ),
-        in_specs=[pl.BlockSpec(memory_space=pltpu.SMEM), vmem, vmem] + [anywhere] * 5,
+        in_specs=[hbm] * 8,
         out_specs=(vmem, vmem, vmem),
         scratch_shapes=[
+            pltpu.SMEM(lengths.shape, jnp.int32),
+            pltpu.VMEM((1, n_dp * slots), jnp.int32),
+            pltpu.VMEM((1, model), BF16),
             pltpu.VMEM((slots, model), BF16),
             pltpu.VMEM((n_dp, slots, wide), BF16),
             pltpu.VMEM((n_dp, slots, wide), BF16),
@@ -304,24 +334,23 @@
             pltpu.VMEM((n_dp, ROWS, LANES), F32),
             pltpu.VMEM((n_all, 2 * ROWS, wide), BF16),
             pltpu.VMEM((n_all, ROWS, LANES), F32),
-            pltpu.VMEM((n_all, ROWS, padded), F32),
-            pltpu.VMEM((n_all, ROWS, padded), F32),
-            pltpu.VMEM((n_vocab, ROWS, wide), F32),
-            dma((5,)),
+            pltpu.VMEM((n_all, ROWS, padded), BF16),
+            pltpu.VMEM((n_all, ROWS, padded), BF16),
+            pltpu.VMEM((n_vocab, ROWS, wide), BF16),
+            dma((8,)),
             dma((n_dp,)), dma((n_dp,)), dma((n_dp,)), dma((n_dp,)),
             dma((n_vocab,)), dma((n_vocab,)), dma((n_vocab,)), dma((n_vocab,)),
             dma((n_dp,)), dma((n_dp,)),
-            dma((n_all,)), dma((n_all,)), dma((n_all,)), dma((n_all,)), dma((n_all,)), dma((n_all,)),
+            dma((n_all // 2,)), dma((n_all // 2,)), dma((n_all // 2,)), dma((n_all // 2,)), dma((n_all,)), dma((n_all,)), dma((n_all,)), dma((n_all,)),
             dma((n_vocab,)), dma((n_vocab,)),
         ],
         compiler_params=pltpu.CompilerParams(
-            collective_id=0, has_side_effects=True, vmem_limit_bytes=40 * 1024 * 1024
+            collective_id=0, has_side_effects=True, vmem_limit_bytes=63 * 1024 * 1024
         ),
     )(lengths, sampled.reshape(1, -1), norm_gain.reshape(1, -1),
       tokens_in, attention, out_projection, tangent, head_weight)
     fisher_product = lax.dot_general(packed, back, (((0,), (0,)), ((), ())), preferred_element_type=F32)
-    token_mine = lax.dynamic_slice_in_dim(token_all[0], lax.axis_index("dp") * live_dev, live_dev)
-    return (fisher_product, token_mine)
+    return (fisher_product, token_mine.reshape(-1))
 
 
 def solution(mesh):

time: 66.8 us -> 50.6 us (0.76)
  Pallas kernels: 53.2 us -> 44.6 us
  local copies, waits for them, and re-layouts: 9.83 us -> 1.82 us
  matrix products: 2.49 us -> 3.35 us
    pallas_call x1, Pallas kernels: 53.2 us -> 44.6 us  [local(): pl.pallas_call(functools.partial(fused_kernel, n_dp, n_vocab), out_shape=...]
    unnamed x14 -> x3, local copies, waits for them, and re-layouts: 8.54 us -> 0.52 us
    dot_general x1, matrix products: 2.49 us -> 3.35 us  [local(): lax.dot_general(packed, back, (((0,), (0,)), ((), ())), preferred_element...]
where the time goes in v2:
time: 50.6 us; the launch traced here: 50.4 us
  Pallas kernels  44.6 us (88%)
  matrix products  3.35 us (7%)
  local copies, waits for them, and re-layouts  1.82 us (4%)
  between operations  0.65 us (1%)
    pallas_call x1, Pallas kernels, local(): pl.pallas_call(functools.partial(fused_kernel, n_dp, n_vocab), out_shape=...  44.6 us
    dot_general x1, matrix products, local(): lax.dot_general(packed, back, (((0,), (0,)), ((), ())), preferred_element...  3.35 us
    reshape x1, local copies, waits for them, and re-layouts, local(): norm_gain.reshape(1, -1)  1.31 us

profile of v2, /device:TPU:0, one launch (start us, length us, event | category | flops | bytes accessed | tf_op | source)
XLA Modules:
  0.0 50.4 jit_solution(2380504104597521750)
XLA Ops:
  0.6 1.3 %reshape.14.gain_hbm = bf16[1,3584]{1,0:T(2,128)(2,1)} reshape(bf16[3584]{0:T(1024)(128)(2,1)} %param.12) | data formatting | bytes 14336 | tf_op jit(solution)/shard_map/reshape | solution.py:350
  1.9 44.6 %shard_map.95 = (bf16[32,1024]{1,0:T(8,128)(2,1)}, bf16[32,896]{1,0:T(8,128)(2,1)}, f32[1,8]{1,0:T(1,128)}) custom-call(s32[4]{0:T(128)} %lengths_hbm.1, s32[1,64]{1,0:T(1,128)} %bitcast.4, bf16[1,3584]{1,0:T(2,128)(2,1)} %reshape.14.gain_hbm, bf16[16,3584]{1,0:T(8,128)(2,1)} %tokens_hbm.1, bf16[16,1024]{1,0:T(8,128)(2,1)} %attention_hbm.1, ...), custom_call_target="tpu_custom_call" | custom-call | tf_op jit(solution)/shard_map/pallas_call | solution.py:309
  46.5 0.0 copy-start
  46.6 3.4 %fusion = f32[1024,896]{1,0:T(8,128)} fusion(bf16[32,1024]{1,0:T(8,128)(2,1)} %get-tuple-element.5, bf16[32,896]{1,0:T(8,128)(2,1)} %get-tuple-element.6), kind=kOutput, calls=%fused_computation | convolution fusion | flops 58720256 | bytes 3792896 | tf_op jit(solution)/shard_map/dot_general | solution.py:352
  49.9 0.0 copy-done
  49.9 0.5 %copy.11 = f32[8]{0:T(128)} copy(f32[8]{0:T(128)S(1)} %bitcast.5) | data formatting | bytes 64
Async XLA Ops:
  46.5 3.4 %copy-start = (f32[1,8]{1,0:T(1,128)S(1)}, f32[1,8]{1,0:T(1,128)}, u32[]{:S(2)}) copy-start(f32[1,8]{1,0:T(1,128)} %get-tuple-element.7) | copy-start | bytes 100

commit v3 on v2

--- a/solution.py
+++ b/solution.py
@@ -81,8 +81,6 @@
     loads[1].wait()
     for block in range(n_dp):
         tokens_send[block] = tokens_own[:, block * wide : (block + 1) * wide]
-    for step in range(1, n_dp):
-        tok_copy(step).start()
     tokens_all[d] = tokens_send[d]
 
     for load in loads[4:7]:
@@ -111,6 +109,8 @@
     loads[0].wait()
     for step in range(1, n_dp):
         att_copy(step).wait()
+    for step in range(1, n_dp):
+        tok_copy(step).start()
     everything = attention_all[...].reshape(n_dp * slots, attention_all.shape[2])
     packed = jnp.dot(pick_narrow, everything, preferred_element_type=F32).astype(BF16)
     packed_ref[...] = packed
@@ -181,48 +181,65 @@
         return copy
 
     def start_all(copy):
-        @pl.loop(1, n_all)
-        def _(step):
-            copy(step).start()
+        if n_all <= 16:
+            for step in range(1, n_all):
+                copy(step).start()
+        else:
+
+            @pl.loop(1, n_all)
+            def _(step):
+                copy(step).start()
 
     def wait_all(copy):
-        @pl.loop(1, n_all)
-        def _(step):
-            copy(step).wait()
+        if n_all <= 16:
+            for step in range(1, n_all):
+                copy(step).wait()
+        else:
+
+            @pl.loop(1, n_all)
+            def _(step):
+                copy(step).wait()
 
     mate = v + 1 - 2 * lax.rem(v, 2)
 
-    def msg_copy(step):
-        _, pd, pv = peer_of(2 * step)
-        return pltpu.make_async_remote_copy(
-            msg_all.at[me], msg_all.at[me], msg_s.at[step], msg_r.at[step],
-            device_id={"dp": pd, "vocab": pv}, device_id_type=MESH)
-
-    def pass_copy(step):
-        came_from = lax.rem(me + n_all - 2 * step, n_all)
-        return pltpu.make_async_remote_copy(
-            msg_all.at[came_from], msg_all.at[came_from], pass_s.at[step], pass_r.at[step],
+    half = n_vocab // 2
+
+    def msg_copy(far, step):
+        slot = far * half + step
+        return pltpu.make_async_remote_copy(
+            msg_all.at[me], msg_all.at[me], msg_s.at[slot], msg_r.at[slot],
+            device_id={"dp": along_dp(far), "vocab": along_vocab(2 * step)}, device_id_type=MESH)
+
+    def pass_copy(far, step):
+        slot = far * half + step
+        came_from = along_dp(n_dp - far) * n_vocab + along_vocab(n_vocab - 2 * step)
+        return pltpu.make_async_remote_copy(
+            msg_all.at[came_from], msg_all.at[came_from], pass_s.at[slot], pass_r.at[slot],
             device_id={"vocab": mate}, device_id_type=MESH)
 
-    for step in range(1, n_all // 2):
-        msg_copy(step).start()
-    pass_copy(0).start()
-    loads[7].wait()
-    for step in range(1, n_all // 2):
-        msg_copy(step).wait_recv()
-        pass_copy(step).start()
-    for step in range(1, n_all // 2):
-        msg_copy(step).wait_send()
-    for step in range(n_all // 2):
-        pass_copy(step).wait()
-
+    hops = [(far, step) for far in range(n_dp) for step in range(half) if far + step > 0]
+    for far, step in hops:
+        msg_copy(far, step).start()
     pair = jnp.zeros((n_vocab * 2 * ROWS, columns), F32)
-    for block in range(n_dp):
+    for far in range(n_dp + 1):
+        if far < n_dp:
+            for step in range(half):
+                if far + step > 0:
+                    msg_copy(far, step).wait_recv()
+                pass_copy(far, step).start()
+        if far == 0:
+            loads[7].wait()
+            continue
+        for step in range(half):
+            pass_copy(far - 1, step).wait()
+        block = along_dp(n_dp - far + 1)
         pair = pair + jnp.dot(
-            msg_all[block * n_vocab : (block + 1) * n_vocab].reshape(n_vocab * 2 * ROWS, wide),
-            head[block * wide : (block + 1) * wide, :],
+            msg_all[pl.ds(block * n_vocab, n_vocab)].reshape(n_vocab * 2 * ROWS, wide),
+            head[pl.ds(pl.multiple_of(block * wide, 32), wide), :],
             preferred_element_type=F32,
         )
+    for far, step in hops:
+        msg_copy(far, step).wait_send()
     pair = pair.reshape(n_vocab, 2 * ROWS, columns)
     logits = pair[:, 0:ROWS].reshape(live, columns)
     squashed = jnp.tanh(logits * (1.0 / SOFT_CAP))
@@ -264,21 +281,31 @@
         + jnp.where(stat_lane == 1, middle, 0.0)
         + jnp.where(stat_lane == 2, low, 0.0)
     ).reshape(n_vocab, ROWS, LANES)
-    for block in range(n_dp):
+    def part_copy(far, step):
+        slot = far * n_vocab + step
+        peer_v = along_vocab(step)
+        return pltpu.make_async_remote_copy(
+            part_send.at[along_dp(far) * n_vocab + peer_v], part_all.at[me], part_s.at[slot], part_r.at[slot],
+            device_id={"dp": along_dp(far), "vocab": peer_v}, device_id_type=MESH)
+
+    for far in [*range(1, n_dp), 0]:
+        block = along_dp(far)
         part = lax.dot_general(
-            back_logits, head[block * wide : (block + 1) * wide, :], NT, preferred_element_type=F32
+            back_logits,
+            head[pl.ds(pl.multiple_of(block * wide, 32), wide), :],
+            NT,
+            preferred_element_type=F32,
         ).reshape(n_vocab, ROWS, wide)
-        part_send[block * n_vocab : (block + 1) * n_vocab, :, 0:wide] = part.astype(BF16)
-        part_send[block * n_vocab : (block + 1) * n_vocab, :, base:] = inner_tail.astype(BF16)
-
-    def part_src(step):
-        peer, _, _ = peer_of(step)
-        return part_send.at[peer]
-
-    part_copy = to_all(part_src, part_all, part_s, part_r)
-    start_all(part_copy)
+        part_send[pl.ds(block * n_vocab, n_vocab), :, 0:wide] = part.astype(BF16)
+        part_send[pl.ds(block * n_vocab, n_vocab), :, base:] = inner_tail.astype(BF16)
+        for step in range(n_vocab):
+            if far + step > 0:
+                part_copy(far, step).start()
     part_all[me] = part_send[me]
-    wait_all(part_copy)
+    for far in range(n_dp):
+        for step in range(n_vocab):
+            if far + step > 0:
+                part_copy(far, step).wait()
     back_gain = gain * jnp.sum(part_all[:, :, 0:wide].astype(F32), axis=0)
     inner_back = jnp.sum(jnp.sum(part_all[:, :, base:].astype(F32), axis=0), axis=1, keepdims=True) * inverse
     bh_all[v] = (scale * back_gain - hidden * (scale * scale * inner_back)).astype(BF16)

time: 50.6 us -> 48.5 us (0.958)
  Pallas kernels: 44.6 us -> 42.5 us
    pallas_call x1, Pallas kernels: 44.6 us -> 42.5 us  [local(): pl.pallas_call(functools.partial(fused_kernel, n_dp, n_vocab), out_shape=...]
where the time goes in v3:
time: 48.5 us; the launch traced here: 48.3 us
  Pallas kernels  42.5 us (88%)
  matrix products  3.35 us (7%)
  local copies, waits for them, and re-layouts  1.82 us (4%)
  between operations  0.65 us (1%)
    pallas_call x1, Pallas kernels, local(): pl.pallas_call(functools.partial(fused_kernel, n_dp, n_vocab), out_shape=...  42.5 us
    dot_general x1, matrix products, local(): lax.dot_general(packed, back, (((0,), (0,)), ((), ())), preferred_element...  3.35 us
    reshape x1, local copies, waits for them, and re-layouts, local(): norm_gain.reshape(1, -1)  1.31 us

profile of v3, /device:TPU:0, one launch (start us, length us, event | category | flops | bytes accessed | tf_op | source)
XLA Modules:
  0.0 48.3 jit_solution(4007838907713948566)
XLA Ops:
  0.6 1.3 %reshape.14.gain_hbm = bf16[1,3584]{1,0:T(2,128)(2,1)} reshape(bf16[3584]{0:T(1024)(128)(2,1)} %param.12) | data formatting | bytes 14336 | tf_op jit(solution)/shard_map/reshape | solution.py:377
  1.9 42.5 %shard_map.95 = (bf16[32,1024]{1,0:T(8,128)(2,1)}, bf16[32,896]{1,0:T(8,128)(2,1)}, f32[1,8]{1,0:T(1,128)}) custom-call(s32[4]{0:T(128)} %lengths_hbm.1, s32[1,64]{1,0:T(1,128)} %bitcast.4, bf16[1,3584]{1,0:T(2,128)(2,1)} %reshape.14.gain_hbm, bf16[16,3584]{1,0:T(8,128)(2,1)} %tokens_hbm.1, bf16[16,1024]{1,0:T(8,128)(2,1)} %attention_hbm.1, ...), custom_call_target="tpu_custom_call" | custom-call | tf_op jit(solution)/shard_map/pallas_call | solution.py:336
  44.5 0.0 copy-start
  44.5 3.4 %fusion = f32[1024,896]{1,0:T(8,128)} fusion(bf16[32,1024]{1,0:T(8,128)(2,1)} %get-tuple-element.5, bf16[32,896]{1,0:T(8,128)(2,1)} %get-tuple-element.6), kind=kOutput, calls=%fused_computation | convolution fusion | flops 58720256 | bytes 3792896 | tf_op jit(solution)/shard_map/dot_general | solution.py:379
  47.8 0.0 copy-done
  47.8 0.5 %copy.11 = f32[8]{0:T(128)} copy(f32[8]{0:T(128)S(1)} %bitcast.5) | data formatting | bytes 64
Async XLA Ops:
  44.5 3.4 %copy-start = (f32[1,8]{1,0:T(1,128)S(1)}, f32[1,8]{1,0:T(1,128)}, u32[]{:S(2)}) copy-start(f32[1,8]{1,0:T(1,128)} %get-tuple-element.7) | copy-start | bytes 100

commit v4 on v3

--- a/solution.py
+++ b/solution.py
@@ -22,9 +22,9 @@
     lengths_hbm, sampled_hbm, gain_hbm, tokens_hbm, attention_hbm, projection_hbm, tangent_hbm, head_hbm,
     packed_ref, back_ref, token_ref,
     lengths_ref, sampled_ref, gain_ref, tokens_own, tokens_send, tokens_all, attention_all, projection, tangent, tangent_narrow, head,
-    hid_send, hid_all, tan_send, tan_all, norm_all, msg_all, stat_all, part_send, part_all, bh_all,
+    hid_send, hid_all, tan_send, tan_all, norm_all, msg_all, stat_all, pair_send, pair_got, part_send, part_all, bh_all,
     local_sem, att_s, att_r, tok_s, tok_r, hid_s, hid_r, tan_s, tan_r, norm_s, norm_r,
-    msg_s, msg_r, pass_s, pass_r, stat_s, stat_r, part_s, part_r, bh_s, bh_r,
+    msg_s, msg_r, pass_s, pass_r, stat_s, stat_r, pair_s, pair_r, part_s, part_r, bh_s, bh_r,
 ):
     d, v = lax.axis_index("dp"), lax.axis_index("vocab")
     n_all = n_dp * n_vocab
@@ -99,9 +99,10 @@
     pick_narrow = pick.astype(BF16)
     wanted = jnp.sum(pick * sampled_ref[...].astype(F32), axis=1, keepdims=True).astype(jnp.int32)
 
+    gain_row = gain_ref[...].astype(F32).reshape(1, model)
     gain = jnp.zeros((1, wide), F32)
     for block in range(n_dp):
-        gain = jnp.where(d == block, gain_ref[:, block * wide : (block + 1) * wide].astype(F32), gain)
+        gain = jnp.where(d == block, gain_row[:, block * wide : (block + 1) * wide], gain)
 
     loads[3].wait()
     tangent_narrow[...] = tangent[...].astype(BF16)
@@ -273,39 +274,59 @@
 
     back_logits = (exp_values / all_total * (tangent_capped - tangent_mean) * slopes).astype(BF16)
     inner_part = jnp.sum(back_logits.astype(F32) * logits, axis=1, keepdims=True)
-    high = inner_part.astype(BF16).astype(F32)
-    middle = (inner_part - high).astype(BF16).astype(F32)
-    low = inner_part - high - middle
-    inner_tail = (
-        jnp.where(stat_lane == 0, high, 0.0)
-        + jnp.where(stat_lane == 1, middle, 0.0)
-        + jnp.where(stat_lane == 2, low, 0.0)
-    ).reshape(n_vocab, ROWS, LANES)
+    inner_tail = jnp.where(stat_lane == 0, inner_part, 0.0).reshape(n_vocab, ROWS, LANES)
+
+    core = lax.rem(v, 2)
+
+    def pair_copy(far, step):
+        slot = far * half + step
+        return pltpu.make_async_remote_copy(
+            pair_send.at[far, 2 * step + 1 - core], pair_got.at[far, step], pair_s.at[slot], pair_r.at[slot],
+            device_id={"vocab": mate}, device_id_type=MESH)
+
     def part_copy(far, step):
-        slot = far * n_vocab + step
-        peer_v = along_vocab(step)
-        return pltpu.make_async_remote_copy(
-            part_send.at[along_dp(far) * n_vocab + peer_v], part_all.at[me], part_s.at[slot], part_r.at[slot],
-            device_id={"dp": along_dp(far), "vocab": peer_v}, device_id_type=MESH)
-
-    for far in [*range(1, n_dp), 0]:
-        block = along_dp(far)
-        part = lax.dot_general(
-            back_logits,
-            head[pl.ds(pl.multiple_of(block * wide, 32), wide), :],
-            NT,
-            preferred_element_type=F32,
-        ).reshape(n_vocab, ROWS, wide)
-        part_send[pl.ds(block * n_vocab, n_vocab), :, 0:wide] = part.astype(BF16)
-        part_send[pl.ds(block * n_vocab, n_vocab), :, base:] = inner_tail.astype(BF16)
-        for step in range(n_vocab):
-            if far + step > 0:
+        slot = far * half + step
+        return pltpu.make_async_remote_copy(
+            part_send.at[slot], part_all.at[slot], part_s.at[slot], part_r.at[slot],
+            device_id={"dp": along_dp(far), "vocab": along_vocab(2 * step)}, device_id_type=MESH)
+
+    order = [*range(1, n_dp), 0]
+    for turn in range(n_dp + 1):
+        if turn < n_dp:
+            far = order[turn]
+            pair_send[far, :, :, 0:wide] = lax.dot_general(
+                back_logits,
+                head[pl.ds(pl.multiple_of(along_dp(far) * wide, 32), wide), :],
+                NT,
+                preferred_element_type=F32,
+            ).reshape(n_vocab, ROWS, wide)
+            pair_send[far, :, :, base:] = inner_tail
+            for step in range(half):
+                pair_copy(far, step).start()
+        if turn == 0:
+            continue
+        far = order[turn - 1]
+        for step in range(half):
+            pair_copy(far, step).wait()
+        for step in range(half):
+            chunk = along_vocab(2 * step)
+            got = pair_got[far, lax.div(chunk, 2)]
+            added = pair_send[far, chunk, :, 0:wide] + got[:, 0:wide]
+            tail = pair_send[far, chunk, :, base:] + got[:, base:]
+            tail = tail[:, 0:1]
+            high = tail.astype(BF16).astype(F32)
+            middle = (tail - high).astype(BF16).astype(F32)
+            tail = jnp.where(lane == 0, high, 0.0) + jnp.where(lane == 1, middle, 0.0) + jnp.where(
+                lane == 2, tail - high - middle, 0.0
+            )
+            slot = far * half + step
+            target = part_send if slot else part_all
+            target[slot, :, 0:wide] = added.astype(BF16)
+            target[slot, :, base:] = tail.astype(BF16)
+            if slot:
                 part_copy(far, step).start()
-    part_all[me] = part_send[me]
-    for far in range(n_dp):
-        for step in range(n_vocab):
-            if far + step > 0:
-                part_copy(far, step).wait()
+    for far, step in hops:
+        part_copy(far, step).wait()
     back_gain = gain * jnp.sum(part_all[:, :, 0:wide].astype(F32), axis=0)
     inner_back = jnp.sum(jnp.sum(part_all[:, :, base:].astype(F32), axis=0), axis=1, keepdims=True) * inverse
     bh_all[v] = (scale * back_gain - hidden * (scale * scale * inner_back)).astype(BF16)
@@ -345,7 +366,7 @@
         scratch_shapes=[
             pltpu.SMEM(lengths.shape, jnp.int32),
             pltpu.VMEM((1, n_dp * slots), jnp.int32),
-            pltpu.VMEM((1, model), BF16),
+            pltpu.VMEM((model,), BF16),
             pltpu.VMEM((slots, model), BF16),
             pltpu.VMEM((n_dp, slots, wide), BF16),
             pltpu.VMEM((n_dp, slots, wide), BF16),
@@ -361,20 +382,24 @@
             pltpu.VMEM((n_dp, ROWS, LANES), F32),
             pltpu.VMEM((n_all, 2 * ROWS, wide), BF16),
             pltpu.VMEM((n_all, ROWS, LANES), F32),
-            pltpu.VMEM((n_all, ROWS, padded), BF16),
-            pltpu.VMEM((n_all, ROWS, padded), BF16),
+            pltpu.VMEM((n_dp, n_vocab, ROWS, padded), F32),
+            pltpu.VMEM((n_dp, n_vocab // 2, ROWS, padded), F32),
+            pltpu.VMEM((n_all // 2, ROWS, padded), BF16),
+            pltpu.VMEM((n_all // 2, ROWS, padded), BF16),
             pltpu.VMEM((n_vocab, ROWS, wide), BF16),
             dma((8,)),
             dma((n_dp,)), dma((n_dp,)), dma((n_dp,)), dma((n_dp,)),
             dma((n_vocab,)), dma((n_vocab,)), dma((n_vocab,)), dma((n_vocab,)),
             dma((n_dp,)), dma((n_dp,)),
-            dma((n_all // 2,)), dma((n_all // 2,)), dma((n_all // 2,)), dma((n_all // 2,)), dma((n_all,)), dma((n_all,)), dma((n_all,)), dma((n_all,)),
+            dma((n_all // 2,)), dma((n_all // 2,)), dma((n_all // 2,)), dma((n_all // 2,)),
+            dma((n_all,)), dma((n_all,)),
+            dma((n_all // 2,)), dma((n_all // 2,)), dma((n_all // 2,)), dma((n_all // 2,)),
             dma((n_vocab,)), dma((n_vocab,)),
         ],
         compiler_params=pltpu.CompilerParams(
             collective_id=0, has_side_effects=True, vmem_limit_bytes=63 * 1024 * 1024
         ),
-    )(lengths, sampled.reshape(1, -1), norm_gain.reshape(1, -1),
+    )(lengths, sampled.reshape(1, -1), norm_gain,
       tokens_in, attention, out_projection, tangent, head_weight)
     fisher_product = lax.dot_general(packed, back, (((0,), (0,)), ((), ())), preferred_element_type=F32)
     return (fisher_product, token_mine.reshape(-1))

time: 48.5 us -> 47.1 us (0.971)
  local copies, waits for them, and re-layouts: 1.82 us -> 0.52 us
    reshape x1 -> x0, local copies, waits for them, and re-layouts: 1.31 us -> none  [local(): norm_gain.reshape(1, -1)]
where the time goes in v4:
time: 47.1 us; the launch traced here: 47 us
  Pallas kernels  42.4 us (90%)
  matrix products  3.35 us (7%)
  between operations  0.65 us (1%)
  local copies, waits for them, and re-layouts  0.52 us (1%)
    pallas_call x1, Pallas kernels, local(): pl.pallas_call(functools.partial(fused_kernel, n_dp, n_vocab), out_shape=...  42.4 us
    dot_general x1, matrix products, local(): lax.dot_general(packed, back, (((0,), (0,)), ((), ())), preferred_element...  3.35 us

profile of v4, /device:TPU:0, one launch (start us, length us, event | category | flops | bytes accessed | tf_op | source)
XLA Modules:
  0.0 47.0 jit_solution(17332902418576928628)
XLA Ops:
  0.6 42.4 %shard_map.95 = (bf16[32,1024]{1,0:T(8,128)(2,1)}, bf16[32,896]{1,0:T(8,128)(2,1)}, f32[1,8]{1,0:T(1,128)}) custom-call(s32[4]{0:T(128)} %lengths_hbm.1, s32[1,64]{1,0:T(1,128)} %bitcast.4, bf16[3584]{0:T(1024)(128)(2,1)} %gain_hbm.1, bf16[16,3584]{1,0:T(8,128)(2,1)} %tokens_hbm.1, bf16[16,1024]{1,0:T(8,128)(2,1)} %attention_hbm.1, ...), custom_call_target="tpu_custom_call" | custom-call | tf_op jit(solution)/shard_map/pallas_call | solution.py:357
  43.1 0.0 copy-start
  43.1 3.4 %fusion = f32[1024,896]{1,0:T(8,128)} fusion(bf16[32,1024]{1,0:T(8,128)(2,1)} %get-tuple-element.5, bf16[32,896]{1,0:T(8,128)(2,1)} %get-tuple-element.6), kind=kOutput, calls=%fused_computation | convolution fusion | flops 58720256 | bytes 3792896 | tf_op jit(solution)/shard_map/dot_general | solution.py:404
  46.4 0.0 copy-done
  46.4 0.5 %copy.11 = f32[8]{0:T(128)} copy(f32[8]{0:T(128)S(1)} %bitcast.5) | data formatting | bytes 64
Async XLA Ops:
  43.1 3.4 %copy-start = (f32[1,8]{1,0:T(1,128)S(1)}, f32[1,8]{1,0:T(1,128)}, u32[]{:S(2)}) copy-start(f32[1,8]{1,0:T(1,128)} %get-tuple-element.7) | copy-start | bytes 100

commit v5 on v4

--- a/solution.py
+++ b/solution.py
@@ -357,8 +357,8 @@
     packed, back, token_mine = pl.pallas_call(
         functools.partial(fused_kernel, n_dp, n_vocab),
         out_shape=(
-            jax.ShapeDtypeStruct((live, features), BF16),
-            jax.ShapeDtypeStruct((live, wide), BF16),
+            pltpu.VMEM((live, features), BF16),
+            pltpu.VMEM((live, wide), BF16),
             jax.ShapeDtypeStruct((1, live_dev), F32),
         ),
         in_specs=[hbm] * 8,
@@ -397,7 +397,7 @@
             dma((n_vocab,)), dma((n_vocab,)),
         ],
         compiler_params=pltpu.CompilerParams(
-            collective_id=0, has_side_effects=True, vmem_limit_bytes=63 * 1024 * 1024
+            collective_id=0, has_side_effects=True, vmem_limit_bytes=60 * 1024 * 1024
         ),
     )(lengths, sampled.reshape(1, -1), norm_gain,
       tokens_in, attention, out_projection, tangent, head_weight)

time: 47.1 us -> 46.1 us (0.979)
  matrix products: 3.35 us -> 2.5 us
    dot_general x1, matrix products: 3.35 us -> 2.5 us  [local(): lax.dot_general(packed, back, (((0,), (0,)), ((), ())), preferred_element...]
where the time goes in v5:
time: 46.1 us; the launch traced here: 46 us
  Pallas kernels  42.3 us (92%)
  matrix products  2.5 us (5%)
  between operations  0.65 us (1%)
  local copies, waits for them, and re-layouts  0.52 us (1%)
    pallas_call x1, Pallas kernels, local(): pl.pallas_call(functools.partial(fused_kernel, n_dp, n_vocab), out_shape=...  42.3 us
    dot_general x1, matrix products, local(): lax.dot_general(packed, back, (((0,), (0,)), ((), ())), preferred_element...  2.5 us

profile of v5, /device:TPU:0, one launch (start us, length us, event | category | flops | bytes accessed | tf_op | source)
XLA Modules:
  0.0 46.0 jit_solution(415164451365394081)
XLA Ops:
  0.6 42.3 %shard_map.95 = (bf16[32,1024]{1,0:T(8,128)(2,1)S(1)}, bf16[32,896]{1,0:T(8,128)(2,1)S(1)}, f32[1,8]{1,0:T(1,128)}) custom-call(s32[4]{0:T(128)} %lengths_hbm.1, s32[1,64]{1,0:T(1,128)} %bitcast.4, bf16[3584]{0:T(1024)(128)(2,1)} %gain_hbm.1, bf16[16,3584]{1,0:T(8,128)(2,1)} %tokens_hbm.1, bf16[16,1024]{1,0:T(8,128)(2,1)} %attention_hbm.1, ...), custom_call_target="tpu_custom_call" | custom-call | tf_op jit(solution)/shard_map/pallas_call | solution.py:357
  43.0 0.0 copy-start
  43.0 2.5 %fusion = f32[1024,896]{1,0:T(8,128)} fusion(bf16[32,1024]{1,0:T(8,128)(2,1)S(1)} %get-tuple-element.5, bf16[32,896]{1,0:T(8,128)(2,1)S(1)} %get-tuple-element.6), kind=kOutput, calls=%fused_computation | convolution fusion | flops 58720256 | bytes 3792896 | tf_op jit(solution)/shard_map/dot_general | solution.py:404
  45.5 0.0 copy-done
  45.5 0.5 %copy.11 = f32[8]{0:T(128)} copy(f32[8]{0:T(128)S(1)} %bitcast.5) | data formatting | bytes 64
Async XLA Ops:
  43.0 2.5 %copy-start = (f32[1,8]{1,0:T(1,128)S(1)}, f32[1,8]{1,0:T(1,128)}, u32[]{:S(2)}) copy-start(f32[1,8]{1,0:T(1,128)} %get-tuple-element.7) | copy-start | bytes 100
